TPU v7x, 256 devices: a whole 4x4x8 slice. The times are simulated.
256 devices in a mesh: frame: 64 (over z, y, core), sector: 4 (over x).
Axes of the slice: x: 4, y: 4, z: 8, core: 2. Of those that a mesh axis runs over, the one named last changes fastest.
Arguments:
- intensity: bfloat16 [1024, 786432], P(('frame', 'sector')), may hold values from 0.099609375 to 10
- block_annulus: int32 [4, 1536], P('sector', 'frame'), may hold values from 0 to 255, as said below
Outputs:
- correlation: float32 [4, 64, 1024, 1024], P('sector', 'frame')
Inputs may be any that keep to these rules, and one draw needn't show every extreme that they name: `block_annulus`: annuli 2k and 2k + 1 together fill the blocks 2k * 24 to (2k + 2) * 24 - 1 of the flattened table, annulus 2k first; every annulus holds 1 to 47 blocks, and some annulus holds exactly 47.
All inputs are finite; a program needn't handle non-finite values.
Results may differ from a plain program's by a relative error of at most 0.0003.
Values may be sent and summed in bfloat16 or wider, within the bound.
No kernel may reach another device: no remote copies, remote signals or barrier semaphores. Data moves between devices by JAX's collectives and lax.ppermute only.
A program may use at most 128 MiB of HBM per device.

v0:
```python
import functools

import jax
import jax.numpy as jnp
from jax import lax
from jax.experimental import pallas as pl
from jax.experimental.pallas import tpu as pltpu
from jax.sharding import PartitionSpec as P

FRAMES = 1024
TILE = 256
PARTS = FRAMES // TILE
HEAD = 16
BLOCKS = 24
QUAD = 4
WIDTH = 128 * QUAD
QUADS = BLOCKS // QUAD
SLOTS = QUADS + 1
GROUP = 2
GROUPS = ((0, 1, 2), (3,))
VMEM = pl.BlockSpec(memory_space=pltpu.VMEM)
SMEM = pl.BlockSpec(memory_space=pltpu.SMEM)
ANY = pl.BlockSpec(memory_space=pl.ANY)


def starts_of(panels):
    starts, row = {}, 0
    for j in panels:
        starts[j] = row
        row += HEAD + TILE * (j + 1)
    return starts, row


def put_in_order(landed, ordered, slot, quad):
    low = lax.broadcasted_iota(jnp.int32, (GROUP, 8, 128), 1) < 4
    for g in range(FRAMES // 16 // GROUP):
        tiles = [
            landed[s, GROUP * g : GROUP * g + GROUP, quad].astype(jnp.float32) for s in range(4)
        ]
        for b in range(QUAD):
            here = [tile[:, 8 * (b // 2) : 8 * (b // 2) + 8] for tile in tiles]
            moved = [pltpu.roll(part, 4, 1) for part in here]
            first, second = (moved, here) if b % 2 else (here, moved)
            halves = [jnp.where(low, first[s], second[s + 1]) for s in (0, 2)]
            block = jnp.concatenate(halves, axis=1).astype(jnp.bfloat16)
            lane = pl.multiple_of(WIDTH * slot + 128 * b, 128)
            row = HEAD + 16 * GROUP * g
            ordered[row : row + 16 * GROUP, pl.ds(lane, 128)] = block.reshape(16 * GROUP, 128)


def gram_kernel(panels, arrives, annulus_ref, *refs):
    if arrives:
        landed, own_ref, other_ref, ordered = refs
    else:
        ordered, own_ref, other_ref = refs
    starts, _ = starts_of(panels)
    number = lax.axis_index("sector") * lax.axis_size("frame") + lax.axis_index("frame")

    def flag(block):
        return jnp.where(annulus_ref[0, block] == number, 1, 0)

    own_blocks = flag(0)
    for b in range(1, BLOCKS):
        own_blocks += flag(b)
    last = (own_blocks + QUAD - 1) // QUAD - 1

    def quad_of(near):
        return jnp.where(number % 2 == 0, near, QUADS - 1 - near)

    if arrives:
        ordered[0:HEAD] = jnp.ones((HEAD, WIDTH * SLOTS), jnp.bfloat16)

        def fill(near, carry):
            slot = jnp.where(near <= last, near, near + 1)
            put_in_order(landed, ordered, slot, quad_of(near))
            return carry

        lax.fori_loop(0, QUADS, fill, 0)
        shared = pl.multiple_of(WIDTH * last, WIDTH)
        after = pl.multiple_of(shared + WIDTH, WIDTH)
        ordered[HEAD:, pl.ds(after, WIDTH)] = ordered[HEAD:, pl.ds(shared, WIDTH)]
        for b in range(QUAD):
            mine = flag(QUAD * quad_of(last) + b)
            lane = pl.multiple_of(jnp.where(mine == 1, after, shared) + 128 * b, 128)
            ordered[HEAD:, pl.ds(lane, 128)] = jnp.zeros((FRAMES, 128), jnp.bfloat16)

    def products(out_ref, low, high):
        for j in panels:
            rows = HEAD + TILE * (j + 1)
            out_ref[starts[j] : starts[j] + rows] = lax.dot_general(
                ordered[0:rows, WIDTH * low : WIDTH * high],
                ordered[HEAD + TILE * j : HEAD + TILE * j + TILE, WIDTH * low : WIDTH * high],
                (((1,), (1,)), ((), ())),
                preferred_element_type=jnp.float32,
            )

    for end in range(QUADS):

        @pl.when(last == end)
        def _(end=end):
            products(own_ref, 0, end + 1)
            products(other_ref, end + 1, SLOTS)

    count = 128.0 * own_blocks.astype(jnp.float32)
    own_ref[8:16] = jnp.full((8, TILE), count, jnp.float32)
    other_ref[8:16] = jnp.full((8, TILE), 128.0 * BLOCKS - count, jnp.float32)


def packed_grams(panels, block_annulus, operand):
    arrives = operand.ndim == 5
    packed = jax.ShapeDtypeStruct((starts_of(panels)[1], TILE), jnp.float32)
    in_order = jax.ShapeDtypeStruct((HEAD + FRAMES, WIDTH * SLOTS), jnp.bfloat16)
    out_shape = (packed, packed, in_order) if arrives else (packed, packed)
    return pl.pallas_call(
        functools.partial(gram_kernel, panels, arrives),
        out_shape=out_shape,
        in_specs=[SMEM, VMEM],
        out_specs=(VMEM,) * len(out_shape),
        compiler_params=pltpu.CompilerParams(vmem_limit_bytes=24 << 20),
        cost_estimate=pl.CostEstimate(
            flops=2 * packed.size * WIDTH * SLOTS, bytes_accessed=6 << 20, transcendentals=0
        ),
        name="grams",
    )(block_annulus, operand)


def finish_kernel(panels, known, groups, *refs):
    own_refs, got_refs, refs = refs[:groups], refs[groups : 2 * groups], refs[2 * groups :]
    out_ref, blocks, copied = refs[-3:]
    place = {
        j: (own_refs[g], got_refs[g], starts_of(GROUPS[g])[0][j])
        for g in range(groups)
        for j in GROUPS[g]
    }

    def total(j, row, rows):
        own_ref, got_ref, start = place[j]
        return own_ref[start + row : start + row + rows] + got_ref[start + row : start + row + rows]

    inverse = {j: 1.0 / total(j, 0, 8)[0:1] for j in known}
    count = total(0, 8, 8)[0:1]

    def column(j):
        half = [
            jnp.transpose(jnp.broadcast_to(inverse[j][:, 128 * k : 128 * k + 128], (128, 128)))
            for k in range(TILE // 128)
        ]
        half = jnp.concatenate(half, axis=0)
        return jnp.concatenate([half, half], axis=1)

    left = {j: column(j) for j in known}
    copies = []

    def send(source_ref, i, j, block):
        rows, columns = slice(TILE * i, TILE * i + TILE), slice(TILE * j, TILE * j + TILE)
        source_ref[rows, columns] = block
        copies.append(
            pltpu.make_async_copy(
                source_ref.at[rows, columns], out_ref.at[rows, columns], copied.at[len(copies)]
            )
        )
        copies[-1].start()

    for j in panels:
        for i in range(j + 1):
            block = total(j, HEAD + TILE * i, TILE) * left[i] * (count * inverse[j])
            send(blocks, i, j, block)
            if i < j:
                send(blocks, j, i, jnp.transpose(block))
    for copy in copies:
        copy.wait()


def finished(own, got):
    out = None
    for g, panels in enumerate(GROUPS):
        known = tuple(range(panels[-1] + 1))
        operands = [*own[: g + 1], *got[: g + 1]] + ([] if out is None else [out])
        copies = sum(2 * j + 1 for j in panels)
        out = pl.pallas_call(
            functools.partial(finish_kernel, panels, known, g + 1),
            out_shape=jax.ShapeDtypeStruct((FRAMES, FRAMES), jnp.float32),
            in_specs=[VMEM] * (2 * g + 2) + ([] if out is None else [ANY]),
            out_specs=ANY,
            input_output_aliases={} if out is None else {2 * g + 2: 0},
            scratch_shapes=[
                pltpu.VMEM((FRAMES, FRAMES), jnp.float32),
                pltpu.SemaphoreType.DMA((copies,)),
            ],
            compiler_params=pltpu.CompilerParams(vmem_limit_bytes=12 << 20),
            cost_estimate=pl.CostEstimate(
                flops=8 << 20, bytes_accessed=4 * TILE * TILE * copies, transcendentals=0
            ),
            name="finish",
        )(*operands)
    return out


def local(intensity, block_annulus):
    devices = lax.axis_size("sector") * lax.axis_size("frame")
    pieces = intensity.reshape(4, devices, BLOCKS, 128).transpose(1, 2, 0, 3)
    arrived = lax.all_to_all(pieces, ("sector", "frame"), split_axis=0, concat_axis=0, tiled=True)
    arrived = arrived.reshape(4, devices // 4, BLOCKS // QUAD, 4 * QUAD, 128)
    return after(arrived, block_annulus)


def after(arrived, block_annulus):
    pairs = [(source, source ^ 1) for source in range(lax.axis_size("frame"))]
    own, got, pixels = [], [], arrived
    for panels in GROUPS:
        mine, other, *in_order = packed_grams(panels, block_annulus, pixels)
        pixels = in_order[0] if in_order else pixels
        own.append(mine)
        got.append(lax.ppermute(other, "frame", pairs))
    return finished(own, got).reshape(1, 1, FRAMES, FRAMES)


def solution(mesh):
    in_specs = (P(("frame", "sector"), None), P("sector", "frame"))
    out_specs = P("sector", "frame", None, None)
    return jax.shard_map(local, mesh=mesh, in_specs=in_specs, out_specs=out_specs, check_vma=False)
```

profile of v0, /device:TPU:1, one launch (start us, length us, event | category | flops | bytes accessed | tf_op | source)
XLA Modules:
  0.0 173.0 jit_solution(18007275154784826595)
XLA Ops:
  0.0 0.0 copy-start
  0.0 158.9 %all_to_all.5 = bf16[256,24,4,128]{3,2,1,0:T(4,128)(2,1)S(1)} all-to-all(bf16[256,24,4,128]{3,2,1,0:T(4,128)(2,1)} %bitcast.6), channel_id=1, replica_groups=mesh['frame'=64,'sector'=4] {'sector','frame'}, dimensions={0} | all-to-all | bytes 12582912 | tf_op jit(solution)/shard_map/all_to_all | solution.py:202
  158.9 0.0 copy-done
  158.9 5.9 %grams.2 = (f32[1584,256]{1,0:T(8,128)S(1)}, f32[1584,256]{1,0:T(8,128)S(1)}, bf16[1040,3584]{1,0:T(8,128)(2,1)S(1)}) custom-call(s32[1,24]{1,0:T(1,128)S(1)} %copy-done, bf16[4,64,6,16,128]{4,3,2,1,0:T(8,128)(2,1)S(1)} %bitcast.5), custom_call_target="tpu_custom_call" | custom-call | flops 2906652672 | bytes 6291456 | tf_op jit(solution)/shard_map/grams/pallas_call | solution.py:114
  164.8 1.1 collective-permute-start
  165.8 2.7 %grams.3 = (f32[1040,256]{1,0:T(8,128)S(1)}, f32[1040,256]{1,0:T(8,128)S(1)}) custom-call(s32[1,24]{1,0:T(1,128)S(1)} %copy-done, bf16[1040,3584]{1,0:T(8,128)(2,1)S(1)} %get-tuple-element.11.refs_0_), custom_call_target="tpu_custom_call" | custom-call | flops 1908408320 | bytes 6291456 | tf_op jit(solution)/shard_map/grams/pallas_call | solution.py:114
  168.6 0.1 collective-permute-start.1
  168.7 0.3 collective-permute-done.refs_1_.refs_2_
  169.0 1.6 finish.2.refs_4_
  170.6 0.8 collective-permute-done.1.refs_3_
  171.4 1.5 finish.3
Async XLA Ops:
  0.0 158.9 %copy-start = (s32[1,24]{1,0:T(1,128)S(1)}, s32[1,24]{1,0:T(1,128)}, u32[]{:S(2)}) copy-start(s32[1,24]{1,0:T(1,128)} %annulus_ref.3) | copy-start | bytes 292
  164.8 4.2 %collective-permute-start = (f32[1584,256]{1,0:T(8,128)S(1)}, f32[1584,256]{1,0:T(8,128)S(1)}, u32[]{:S(2)}, u32[]{:S(2)}) collective-permute-start(f32[1584,256]{1,0:T(8,128)S(1)} %get-tuple-element.13), channel_id=1, source_target_pairs={{0,4},{4,0},{8,12},{12,8},{16,20},{20,16},{24,28},{28,24},{32,36},... | collective-permute-start | bytes 4866056 | tf_op jit(solution)/shard_map/ppermute | solution.py:214
  168.6 2.8 %collective-permute-start.1 = (f32[1040,256]{1,0:T(8,128)S(1)}, f32[1040,256]{1,0:T(8,128)S(1)}, u32[]{:S(2)}, u32[]{:S(2)}) collective-permute-start(f32[1040,256]{1,0:T(8,128)S(1)} %get-tuple-element.14), channel_id=1, source_target_pairs={{0,4},{4,0},{8,12},{12,8},{16,20},{20,16},{24,28},{28,24},{32,36},... | collective-permute-start | bytes 3194888 | tf_op jit(solution)/shard_map/ppermute | solution.py:214
where the time goes:
time: 173 us
  blocking collectives  159 us (92%)
  Pallas kernels  11.7 us (7%)
    all_to_all x1, blocking collectives, local(): lax.all_to_all(pieces, ('sector', 'frame'), split_axis=0, concat_axis=0,...  159 us
    pallas_call x2, Pallas kernels, packed_grams(): pl.pallas_call(functools.partial(gram_kernel, panels, arrives), out_shape...  8.62 us
  transfers between devices with their start and end apart: 2, of which 2 were waited for; matrix products, arithmetic and copies ran while one was open for 0% of the time, Pallas kernels for 3%

commit v1 on v0

--- a/solution.py
+++ b/solution.py
@@ -19,7 +19,6 @@
 GROUP = 2
 GROUPS = ((0, 1, 2), (3,))
 VMEM = pl.BlockSpec(memory_space=pltpu.VMEM)
-SMEM = pl.BlockSpec(memory_space=pltpu.SMEM)
 ANY = pl.BlockSpec(memory_space=pl.ANY)
 
 
@@ -56,12 +55,7 @@
     starts, _ = starts_of(panels)
     number = lax.axis_index("sector") * lax.axis_size("frame") + lax.axis_index("frame")
 
-    def flag(block):
-        return jnp.where(annulus_ref[0, block] == number, 1, 0)
-
-    own_blocks = flag(0)
-    for b in range(1, BLOCKS):
-        own_blocks += flag(b)
+    own_blocks = jnp.sum(jnp.where(annulus_ref[...] == number, 1.0, 0.0)).astype(jnp.int32)
     last = (own_blocks + QUAD - 1) // QUAD - 1
 
     def quad_of(near):
@@ -70,18 +64,16 @@
     if arrives:
         ordered[0:HEAD] = jnp.ones((HEAD, WIDTH * SLOTS), jnp.bfloat16)
 
-        def fill(near, carry):
-            slot = jnp.where(near <= last, near, near + 1)
+        for near in range(QUADS):
+            slot = jnp.where(near <= last, near, near + 1) if near else 0
             put_in_order(landed, ordered, slot, quad_of(near))
-            return carry
-
-        lax.fori_loop(0, QUADS, fill, 0)
-        shared = pl.multiple_of(WIDTH * last, WIDTH)
-        after = pl.multiple_of(shared + WIDTH, WIDTH)
-        ordered[HEAD:, pl.ds(after, WIDTH)] = ordered[HEAD:, pl.ds(shared, WIDTH)]
+
+    def split(end):
+        shared, after = WIDTH * end, WIDTH * (end + 1)
+        ordered[HEAD:, after : after + WIDTH] = ordered[HEAD:, shared : shared + WIDTH]
         for b in range(QUAD):
-            mine = flag(QUAD * quad_of(last) + b)
-            lane = pl.multiple_of(jnp.where(mine == 1, after, shared) + 128 * b, 128)
+            place = QUAD * end + jnp.where(number % 2 == 0, b, QUAD - 1 - b)
+            lane = pl.multiple_of(jnp.where(place < own_blocks, after, shared) + 128 * b, 128)
             ordered[HEAD:, pl.ds(lane, 128)] = jnp.zeros((FRAMES, 128), jnp.bfloat16)
 
     def products(out_ref, low, high):
@@ -98,6 +90,8 @@
 
         @pl.when(last == end)
         def _(end=end):
+            if arrives:
+                split(end)
             products(own_ref, 0, end + 1)
             products(other_ref, end + 1, SLOTS)
 
@@ -114,7 +108,7 @@
     return pl.pallas_call(
         functools.partial(gram_kernel, panels, arrives),
         out_shape=out_shape,
-        in_specs=[SMEM, VMEM],
+        in_specs=[VMEM, VMEM],
         out_specs=(VMEM,) * len(out_shape),
         compiler_params=pltpu.CompilerParams(vmem_limit_bytes=24 << 20),
         cost_estimate=pl.CostEstimate(

time: 173 us -> 172 us (level)
  transfers between devices with their start and end apart: 2 -> 2, of which waited for: 2 -> 2; matrix products, arithmetic and copies ran while one was open for 0% -> 0% of each run, Pallas kernels for 3% -> 2%
where the time goes in v1:
time: 172 us
  blocking collectives  159 us (92%)
  Pallas kernels  10.7 us (6%)
    all_to_all x1, blocking collectives, local(): lax.all_to_all(pieces, ('sector', 'frame'), split_axis=0, concat_axis=0,...  159 us
    pallas_call x2, Pallas kernels, packed_grams(): pl.pallas_call(functools.partial(gram_kernel, panels, arrives), out_shape...  7.62 us
  transfers between devices with their start and end apart: 2, of which 2 were waited for; matrix products, arithmetic and copies ran while one was open for 0% of the time, Pallas kernels for 2%

profile of v1, /device:TPU:1, one launch (start us, length us, event | category | flops | bytes accessed | tf_op | source)
XLA Modules:
  0.0 172.0 jit_solution(12571956293892013640)
XLA Ops:
  0.0 0.0 copy-start
  0.0 158.9 %all_to_all.5 = bf16[256,24,4,128]{3,2,1,0:T(4,128)(2,1)S(1)} all-to-all(bf16[256,24,4,128]{3,2,1,0:T(4,128)(2,1)} %bitcast.6), channel_id=1, replica_groups=mesh['frame'=64,'sector'=4] {'sector','frame'}, dimensions={0} | all-to-all | bytes 12582912 | tf_op jit(solution)/shard_map/all_to_all | solution.py:196
  158.9 0.0 copy-done
  158.9 5.1 %grams.2 = (f32[1584,256]{1,0:T(8,128)S(1)}, f32[1584,256]{1,0:T(8,128)S(1)}, bf16[1040,3584]{1,0:T(8,128)(2,1)S(1)}) custom-call(s32[1,24]{1,0:T(1,128)S(1)} %copy-done, bf16[4,64,6,16,128]{4,3,2,1,0:T(8,128)(2,1)S(1)} %bitcast.5), custom_call_target="tpu_custom_call" | custom-call | flops 2906652672 | bytes 6291456 | tf_op jit(solution)/shard_map/grams/pallas_call | solution.py:108
  164.0 1.1 collective-permute-start
  165.1 2.5 %grams.3 = (f32[1040,256]{1,0:T(8,128)S(1)}, f32[1040,256]{1,0:T(8,128)S(1)}) custom-call(s32[1,24]{1,0:T(1,128)S(1)} %copy-done, bf16[1040,3584]{1,0:T(8,128)(2,1)S(1)} %get-tuple-element.11.refs_0_), custom_call_target="tpu_custom_call" | custom-call | flops 1908408320 | bytes 6291456 | tf_op jit(solution)/shard_map/grams/pallas_call | solution.py:108
  167.6 0.1 collective-permute-start.1
  167.7 0.5 collective-permute-done.refs_1_.refs_2_
  168.2 1.6 finish.2.refs_4_
  169.8 0.6 collective-permute-done.1.refs_3_
  170.4 1.5 finish.3
Async XLA Ops:
  0.0 158.9 %copy-start = (s32[1,24]{1,0:T(1,128)S(1)}, s32[1,24]{1,0:T(1,128)}, u32[]{:S(2)}) copy-start(s32[1,24]{1,0:T(1,128)} %annulus_ref.3) | copy-start | bytes 292
  164.0 4.2 %collective-permute-start = (f32[1584,256]{1,0:T(8,128)S(1)}, f32[1584,256]{1,0:T(8,128)S(1)}, u32[]{:S(2)}, u32[]{:S(2)}) collective-permute-start(f32[1584,256]{1,0:T(8,128)S(1)} %get-tuple-element.13), channel_id=1, source_target_pairs={{0,4},{4,0},{8,12},{12,8},{16,20},{20,16},{24,28},{28,24},{32,36},... | collective-permute-start | bytes 4866056 | tf_op jit(solution)/shard_map/ppermute | solution.py:208
  167.6 2.8 %collective-permute-start.1 = (f32[1040,256]{1,0:T(8,128)S(1)}, f32[1040,256]{1,0:T(8,128)S(1)}, u32[]{:S(2)}, u32[]{:S(2)}) collective-permute-start(f32[1040,256]{1,0:T(8,128)S(1)} %get-tuple-element.14), channel_id=1, source_target_pairs={{0,4},{4,0},{8,12},{12,8},{16,20},{20,16},{24,28},{28,24},{32,36},... | collective-permute-start | bytes 3194888 | tf_op jit(solution)/shard_map/ppermute | solution.py:208

commit v2 on v1

--- a/solution.py
+++ b/solution.py
@@ -11,6 +11,8 @@
 TILE = 256
 PARTS = FRAMES // TILE
 HEAD = 16
+SUMS = 8
+HALF = TILE // 2
 BLOCKS = 24
 QUAD = 4
 WIDTH = 128 * QUAD
@@ -26,7 +28,7 @@
     starts, row = {}, 0
     for j in panels:
         starts[j] = row
-        row += HEAD + TILE * (j + 1)
+        row += SUMS + TILE * j + TILE * 3 // 4
     return starts, row
 
 
@@ -79,12 +81,18 @@
     def products(out_ref, low, high):
         for j in panels:
             rows = HEAD + TILE * (j + 1)
-            out_ref[starts[j] : starts[j] + rows] = lax.dot_general(
+            panel = lax.dot_general(
                 ordered[0:rows, WIDTH * low : WIDTH * high],
                 ordered[HEAD + TILE * j : HEAD + TILE * j + TILE, WIDTH * low : WIDTH * high],
                 (((1,), (1,)), ((), ())),
                 preferred_element_type=jnp.float32,
             )
+            folded = starts[j] + SUMS + TILE * j + HALF
+            out_ref[starts[j] : folded] = panel[HEAD - SUMS : rows - HALF]
+            for k in range(2):
+                out_ref[folded : folded + HALF // 2, HALF * k : HALF * k + HALF] = panel[
+                    rows - HALF + HALF // 2 * k : rows - HALF + HALF // 2 * (k + 1), HALF:
+                ]
 
     for end in range(QUADS):
 
@@ -96,8 +104,8 @@
             products(other_ref, end + 1, SLOTS)
 
     count = 128.0 * own_blocks.astype(jnp.float32)
-    own_ref[8:16] = jnp.full((8, TILE), count, jnp.float32)
-    other_ref[8:16] = jnp.full((8, TILE), 128.0 * BLOCKS - count, jnp.float32)
+    own_ref[SUMS - 1 : SUMS] = jnp.full((1, TILE), count, jnp.float32)
+    other_ref[SUMS - 1 : SUMS] = jnp.full((1, TILE), 128.0 * BLOCKS - count, jnp.float32)
 
 
 def packed_grams(panels, block_annulus, operand):
@@ -131,8 +139,8 @@
         own_ref, got_ref, start = place[j]
         return own_ref[start + row : start + row + rows] + got_ref[start + row : start + row + rows]
 
-    inverse = {j: 1.0 / total(j, 0, 8)[0:1] for j in known}
-    count = total(0, 8, 8)[0:1]
+    inverse = {j: 1.0 / total(j, 0, 1) for j in known}
+    count = total(0, SUMS - 1, 1)
 
     def column(j):
         half = [
@@ -155,9 +163,18 @@
         )
         copies[-1].start()
 
+    def products(i, j):
+        if i < j:
+            return total(j, SUMS + TILE * i, TILE)
+        upper = total(j, SUMS + TILE * j, HALF)
+        folded = total(j, SUMS + TILE * j + HALF, HALF // 2)
+        right = jnp.concatenate([folded[:, :HALF], folded[:, HALF:]], axis=0)
+        lower = jnp.concatenate([jnp.transpose(upper[:, HALF:]), right], axis=1)
+        return jnp.concatenate([upper, lower], axis=0)
+
     for j in panels:
         for i in range(j + 1):
-            block = total(j, HEAD + TILE * i, TILE) * left[i] * (count * inverse[j])
+            block = products(i, j) * left[i] * (count * inverse[j])
             send(blocks, i, j, block)
             if i < j:
                 send(blocks, j, i, jnp.transpose(block))

time: 172 us -> 172 us (level)
  no operation moved by 1% of the time
where the time goes in v2:
time: 172 us
  blocking collectives  159 us (92%)
  Pallas kernels  10.8 us (6%)
    all_to_all x1, blocking collectives, local(): lax.all_to_all(pieces, ('sector', 'frame'), split_axis=0, concat_axis=0,...  159 us
    pallas_call x2, Pallas kernels, packed_grams(): pl.pallas_call(functools.partial(gram_kernel, panels, arrives), out_shape...  7.61 us
  transfers between devices with their start and end apart: 2, of which 2 were waited for; matrix products, arithmetic and copies ran while one was open for 0% of the time, Pallas kernels for 2%

profile of v2, /device:TPU:1, one launch (start us, length us, event | category | flops | bytes accessed | tf_op | source)
XLA Modules:
  0.0 172.0 jit_solution(3051889383384164398)
XLA Ops:
  0.0 0.0 copy-start
  0.0 158.9 %all_to_all.5 = bf16[256,24,4,128]{3,2,1,0:T(4,128)(2,1)S(1)} all-to-all(bf16[256,24,4,128]{3,2,1,0:T(4,128)(2,1)} %bitcast.6), channel_id=1, replica_groups=mesh['frame'=64,'sector'=4] {'sector','frame'}, dimensions={0} | all-to-all | bytes 12582912 | tf_op jit(solution)/shard_map/all_to_all | solution.py:213
  158.9 0.0 copy-done
  158.9 5.1 %grams.2 = (f32[1368,256]{1,0:T(8,128)S(1)}, f32[1368,256]{1,0:T(8,128)S(1)}, bf16[1040,3584]{1,0:T(8,128)(2,1)S(1)}) custom-call(s32[1,24]{1,0:T(1,128)S(1)} %copy-done, bf16[4,64,6,16,128]{4,3,2,1,0:T(8,128)(2,1)S(1)} %bitcast.5), custom_call_target="tpu_custom_call" | custom-call | flops 2510290944 | bytes 6291456 | tf_op jit(solution)/shard_map/grams/pallas_call | solution.py:116
  164.0 1.2 collective-permute-start
  165.2 2.5 %grams.3 = (f32[968,256]{1,0:T(8,128)S(1)}, f32[968,256]{1,0:T(8,128)S(1)}) custom-call(s32[1,24]{1,0:T(1,128)S(1)} %copy-done, bf16[1040,3584]{1,0:T(8,128)(2,1)S(1)} %get-tuple-element.11.refs_0_), custom_call_target="tpu_custom_call" | custom-call | flops 1776287744 | bytes 6291456 | tf_op jit(solution)/shard_map/grams/pallas_call | solution.py:116
  167.7 0.1 collective-permute-start.1
  167.8 0.2 collective-permute-done.refs_1_.refs_2_
  168.0 1.7 finish.2.refs_4_
  169.7 0.7 collective-permute-done.1.refs_3_
  170.4 1.5 finish.3
Async XLA Ops:
  0.0 158.9 %copy-start = (s32[1,24]{1,0:T(1,128)S(1)}, s32[1,24]{1,0:T(1,128)}, u32[]{:S(2)}) copy-start(s32[1,24]{1,0:T(1,128)} %annulus_ref.3) | copy-start | bytes 292
  164.0 4.0 %collective-permute-start = (f32[1368,256]{1,0:T(8,128)S(1)}, f32[1368,256]{1,0:T(8,128)S(1)}, u32[]{:S(2)}, u32[]{:S(2)}) collective-permute-start(f32[1368,256]{1,0:T(8,128)S(1)} %get-tuple-element.13), channel_id=1, source_target_pairs={{0,4},{4,0},{8,12},{12,8},{16,20},{20,16},{24,28},{28,24},{32,36},... | collective-permute-start | bytes 4202504 | tf_op jit(solution)/shard_map/ppermute | solution.py:225
  167.7 2.7 %collective-permute-start.1 = (f32[968,256]{1,0:T(8,128)S(1)}, f32[968,256]{1,0:T(8,128)S(1)}, u32[]{:S(2)}, u32[]{:S(2)}) collective-permute-start(f32[968,256]{1,0:T(8,128)S(1)} %get-tuple-element.14), channel_id=1, source_target_pairs={{0,4},{4,0},{8,12},{12,8},{16,20},{20,16},{24,28},{28,24},{32,36},... | collective-permute-start | bytes 2973704 | tf_op jit(solution)/shard_map/ppermute | solution.py:225
